TPU v7x, 32 devices: a whole 2x2x4 slice. The times are simulated.
32 devices in a mesh: ctx: 16 (over z, x, core), batch: 2 (over y).
Axes of the slice: x: 2, y: 2, z: 4, core: 2. Of those that a mesh axis runs over, the one named last changes fastest.
Arguments:
- mixer_input: bfloat16 [2, 2048, 10240], P('batch', 'ctx'), may hold values from -6 to 6
- z_gate: bfloat16 [2, 2048, 8192], P('batch', 'ctx'), may hold values from -6 to 6
- time_step: bfloat16 [2, 2048, 128], P('batch', 'ctx'), may hold values from -4.5 to 0.5
- conv_weight: float32 [4, 10240], replicated, may hold values from -3 to 3
- conv_bias: float32 [10240], replicated, may hold values from -3 to 3
- decay_rate: float32 [128], replicated, may hold values from 0.000146484375 to 0.25
- skip_gain: float32 [128], replicated, may hold values from 0.3 to 1.5
- norm_gain: float32 [8192], replicated, may hold values from 0.5 to 1.5
- doc_lengths: int32 [2, 6], replicated, may hold values from 1 to 1536, 2048 in all within a row
- queries: bfloat16 [2, 2048, 4096], P('batch', 'ctx'), may hold values from -101.6466 to 101.6466
- attn_keys: bfloat16 [2, 2048, 1024], P('batch', 'ctx'), may hold values from -5 to 5
- attn_values: bfloat16 [2, 2048, 1024], P('batch', 'ctx'), may hold values from -6 to 6
Outputs:
- mixer_out: bfloat16 [2, 2048, 8192], P('batch', 'ctx')
- attn_out: bfloat16 [2, 2048, 4096], P('batch', 'ctx')
Inputs may be any that keep to these rules, and one draw needn't show every extreme that they name: `doc_lengths`: each sequence's 6 lengths sum to 2048, and the longest is exactly 1536.
All inputs are finite; a program needn't handle non-finite values.
Results may differ from a plain program's by a relative error of at most 0.011.
Values may be sent and summed in bfloat16 or wider, within the bound.
A program may use at most 256 MiB of HBM per device.

v0:
```python
import jax
import jax.numpy as jnp
from jax import lax
from jax.sharding import PartitionSpec as P

HEADS = 128
HEAD_DIM = 64
STATE = 128
GROUPS = 8
QHEADS = 32
KVHEADS = 8
QDIM = 128
STRETCH = 128
WINDOW = 2048


EPSILON = 1e-05
NEGATIVE = -1e30


def segment_ids(doc_lengths, positions):
    endings = jnp.cumsum(doc_lengths, axis=-1, dtype=jnp.int32)
    starting = endings - doc_lengths
    return (
        jnp.sum(
            (starting[:, None, :] <= positions[None, :, None]).astype(jnp.int32),
            axis=-1,
            dtype=jnp.int32,
        )
        - 1
    )


def causal_conv(inputs, conv_weight, conv_bias, segments, rim_rows, rim_segments):
    padded = jnp.concatenate([rim_rows, inputs], axis=1).astype(jnp.float32)
    padded_seg = jnp.concatenate([rim_segments, segments], axis=1)
    length = inputs.shape[1]
    kernel_taps = conv_weight.shape[0]
    summed = jnp.zeros(inputs.shape, jnp.float32) + conv_bias
    for offset in range(kernel_taps):
        window_rows = padded[:, offset : offset + length]
        matches = (padded_seg[:, offset : offset + length] == segments)[..., None]
        summed = summed + jnp.where(matches, window_rows * conv_weight[offset], 0.0)
    return jax.nn.silu(summed).astype(jnp.bfloat16)


def ssd_block(carried_in, pieces, decay_rates, skip_gains):
    state_now, prev_seg = carried_in
    head_inputs, step_sizes, input_proj, output_proj, segments = pieces
    log_decay = jnp.cumsum(-step_sizes * decay_rates, axis=1)
    block_len = segments.shape[1]
    position = jnp.arange(block_len, dtype=jnp.int32)
    related = (segments[:, :, None] == segments[:, None, :]) & (
        position[:, None] >= position[None, :]
    )
    spread = log_decay[:, :, None] - log_decay[:, None, :]
    decays = jnp.where(related[..., None, None], jnp.exp(jnp.minimum(spread, 0.0)), 0.0)
    scores = jnp.einsum(
        "sqgn,skgn->sqkg", output_proj, input_proj, preferred_element_type=jnp.float32
    )
    weights = (scores[..., None] * decays * step_sizes[:, None]).astype(jnp.bfloat16)
    inner_part = jnp.einsum(
        "sqkgr,skgrp->sqgrp", weights, head_inputs, preferred_element_type=jnp.float32
    )
    carried = jnp.einsum(
        "sqgn,sgrnp->sqgrp",
        output_proj.astype(jnp.float32),
        state_now,
        precision=lax.Precision.HIGHEST,
    )
    keep_rows = (segments == prev_seg[:, None])[:, :, None, None]
    between = jnp.where(keep_rows, jnp.exp(log_decay), 0.0)[..., None] * carried
    outputs = inner_part + between + skip_gains[..., None] * head_inputs.astype(jnp.float32)
    last_seg = segments[:, -1]
    trailing = jnp.where(
        (segments == last_seg[:, None])[:, :, None, None],
        jnp.exp(log_decay[:, -1:] - log_decay) * step_sizes,
        0.0,
    )
    fresh_state = jnp.einsum(
        "sqgn,sqgrp->sgrnp",
        input_proj.astype(jnp.float32),
        trailing[..., None] * head_inputs.astype(jnp.float32),
        precision=lax.Precision.HIGHEST,
    )
    through = jnp.where((last_seg == prev_seg)[:, None, None], jnp.exp(log_decay[:, -1]), 0.0)
    return ((through[..., None, None] * state_now + fresh_state, last_seg), outputs)


def run_blocks(
    head_inputs, step_sizes, input_proj, output_proj, segments, decay_rates, skip_gains, block_len
):
    num_seqs, length = segments.shape
    state_zero = jnp.zeros(
        (num_seqs,) + head_inputs.shape[2:4] + (input_proj.shape[-1], head_inputs.shape[-1]),
        jnp.float32,
    )
    prev_zero = jnp.full((num_seqs,), -1, jnp.int32)

    def run_advance(carried_in, block_index):
        block_start = block_index * block_len
        pieces = tuple(
            (
                lax.dynamic_slice_in_dim(array_in, block_start, block_len, 1)
                for array_in in (head_inputs, step_sizes, input_proj, output_proj, segments)
            )
        )
        return ssd_block(carried_in, pieces, decay_rates, skip_gains)

    final_carry, outputs = lax.scan(
        run_advance, (state_zero, prev_zero), jnp.arange(length // block_len, dtype=jnp.int32)
    )
    return (final_carry[0], jnp.moveaxis(outputs, 0, 1).reshape(head_inputs.shape))


def gated_norm(mixed, z_gate, norm_gain):
    gated = mixed.astype(jnp.float32) * jax.nn.silu(z_gate.astype(jnp.float32))
    grouped = gated.reshape(gated.shape[:-1] + (GROUPS, gated.shape[-1] // GROUPS))
    scaling = lax.rsqrt(jnp.mean(grouped * grouped, axis=-1, keepdims=True) + EPSILON)
    return ((grouped * scaling).reshape(gated.shape) * norm_gain).astype(jnp.bfloat16)


def on_device(
    mixer_input,
    z_gate,
    time_step,
    conv_weight,
    conv_bias,
    decay_rate,
    skip_gain,
    norm_gain,
    doc_lengths,
    queries,
    attn_keys,
    attn_values,
):
    local_rows = mixer_input.shape[1]
    ctx_count = lax.axis_size("ctx")
    batch_count = lax.axis_size("batch")
    ctx_rank = lax.axis_index("ctx")
    batch_rank = lax.axis_index("batch")
    inner_width = HEADS * HEAD_DIM
    proj_width = GROUPS * STATE
    kernel_taps = conv_weight.shape[0]
    first_row = ctx_rank * local_rows
    local_pos = first_row + jnp.arange(local_rows, dtype=jnp.int32)
    own_lengths = lax.dynamic_slice_in_dim(doc_lengths, batch_rank, 1, 0)
    local_seg = segment_ids(own_lengths, local_pos)
    seq_len = local_rows * ctx_count
    per_device = HEADS // (ctx_count * batch_count)
    first_head = batch_rank * (HEADS // batch_count) + ctx_rank * per_device
    group_global = first_head // (HEADS // GROUPS)
    group_local = group_global - batch_rank * (GROUPS // batch_count)
    head_raw, step_raw = (
        lax.all_to_all(
            lax.all_to_all(
                mixer_input[:, :, :inner_width], "batch", split_axis=2, concat_axis=0, tiled=True
            ),
            "ctx",
            split_axis=2,
            concat_axis=1,
            tiled=True,
        ),
        lax.all_to_all(
            lax.all_to_all(time_step, "batch", split_axis=2, concat_axis=0, tiled=True),
            "ctx",
            split_axis=2,
            concat_axis=1,
            tiled=True,
        ),
    )
    proj_raw = mixer_input[:, :, inner_width:].reshape(1, local_rows, 2, GROUPS, STATE)
    group_rows = lax.all_to_all(proj_raw, "batch", split_axis=3, concat_axis=0, tiled=True)
    whole_proj = lax.all_gather(group_rows, "ctx", axis=1, tiled=True)
    own_proj = lax.dynamic_slice_in_dim(whole_proj, group_local, 1, 3).reshape(
        batch_count, seq_len, 2 * STATE
    )
    input_cols = inner_width + group_global * STATE
    output_cols = inner_width + proj_width + group_global * STATE
    proj_weight = jnp.concatenate(
        [
            lax.dynamic_slice_in_dim(conv_weight, input_cols, STATE, 1),
            lax.dynamic_slice_in_dim(conv_weight, output_cols, STATE, 1),
        ],
        axis=1,
    )
    proj_bias = jnp.concatenate(
        [
            lax.dynamic_slice_in_dim(conv_bias, input_cols, STATE, 0),
            lax.dynamic_slice_in_dim(conv_bias, output_cols, STATE, 0),
        ],
        axis=0,
    )
    all_seg = segment_ids(doc_lengths, jnp.arange(seq_len, dtype=jnp.int32))
    rim_segments = jnp.full((batch_count, kernel_taps - 1), -1, jnp.int32)
    proj_act = causal_conv(
        own_proj,
        proj_weight,
        proj_bias,
        all_seg,
        jnp.zeros((batch_count, kernel_taps - 1, 2 * STATE), jnp.bfloat16),
        rim_segments,
    )
    head_weight = lax.dynamic_slice_in_dim(
        conv_weight, first_head * HEAD_DIM, per_device * HEAD_DIM, 1
    )
    head_bias = lax.dynamic_slice_in_dim(conv_bias, first_head * HEAD_DIM, per_device * HEAD_DIM, 0)
    head_act = causal_conv(
        head_raw,
        head_weight,
        head_bias,
        all_seg,
        jnp.zeros((batch_count, kernel_taps - 1, per_device * HEAD_DIM), jnp.bfloat16),
        rim_segments,
    )
    step_sizes = jax.nn.softplus(step_raw.astype(jnp.float32)).reshape(
        batch_count, seq_len, 1, per_device
    )
    head_rates = lax.dynamic_slice_in_dim(decay_rate, first_head, per_device, 0).reshape(
        1, per_device
    )
    head_skips = lax.dynamic_slice_in_dim(skip_gain, first_head, per_device, 0).reshape(
        1, per_device
    )
    final_state, mixed_heads = run_blocks(
        head_act.reshape(batch_count, seq_len, 1, per_device, HEAD_DIM),
        step_sizes,
        proj_act[:, :, :STATE].reshape(batch_count, seq_len, 1, STATE),
        proj_act[:, :, STATE:].reshape(batch_count, seq_len, 1, STATE),
        all_seg,
        head_rates,
        head_skips,
        STRETCH,
    )
    mixed_send = mixed_heads.astype(jnp.bfloat16).reshape(
        batch_count, seq_len, per_device * HEAD_DIM
    )
    mixed = lax.all_to_all(
        lax.all_to_all(mixed_send, "ctx", split_axis=1, concat_axis=2, tiled=True),
        "batch",
        split_axis=0,
        concat_axis=2,
        tiled=True,
    )
    mixer_out = gated_norm(mixed, z_gate, norm_gain)
    group_size = QHEADS // KVHEADS
    scaling = QDIM ** (-0.5)
    query_rows = queries[0].reshape(local_rows, KVHEADS, group_size, QDIM)
    row_seg = local_seg[0]

    def attend_rows(carry_in, key_rows, value_rows, key_start):
        high_now, total_now, accum_now = carry_in
        key_count = key_rows.shape[0]
        key_pos = key_start + jnp.arange(key_count, dtype=jnp.int32)
        key_seg = segment_ids(own_lengths, key_pos)
        visible = (
            (key_seg == row_seg[:, None])
            & (key_pos[None, :] <= local_pos[:, None])
            & (local_pos[:, None] - key_pos[None, :] < WINDOW)
        )
        scores = (
            jnp.einsum(
                "qkgd,rkd->kgqr",
                query_rows,
                key_rows.reshape(key_count, KVHEADS, QDIM),
                preferred_element_type=jnp.float32,
            )
            * scaling
        )
        masked = jnp.where(visible, scores, NEGATIVE)
        high_next = jnp.maximum(high_now, jnp.max(masked, axis=-1))
        numerators = jnp.where(visible, jnp.exp(masked - high_next[..., None]), 0.0)
        fading = jnp.exp(high_now - high_next)
        total_next = total_now * fading + jnp.sum(numerators, axis=-1)
        accum_next = accum_now * jnp.moveaxis(fading, -1, 0)[..., None] + jnp.einsum(
            "kgqr,rkd->qkgd",
            numerators.astype(jnp.bfloat16),
            value_rows.reshape(key_count, KVHEADS, QDIM),
            preferred_element_type=jnp.float32,
        )
        return (high_next, total_next, accum_next)

    initial = (
        jnp.full((KVHEADS, group_size, local_rows), NEGATIVE, jnp.float32),
        jnp.zeros((KVHEADS, group_size, local_rows), jnp.float32),
        jnp.zeros((local_rows, KVHEADS, group_size, QDIM), jnp.float32),
    )
    key_piece = lax.all_gather(attn_keys[0], "ctx", axis=0, tiled=True)
    value_piece = lax.all_gather(attn_values[0], "ctx", axis=0, tiled=True)
    piece_rows = key_piece.shape[0]
    step_rows = 512

    def sweep_advance(carry_inner, block_index):
        offset = block_index * step_rows
        updated = attend_rows(
            carry_inner,
            lax.dynamic_slice_in_dim(key_piece, offset, step_rows, 0),
            lax.dynamic_slice_in_dim(value_piece, offset, step_rows, 0),
            offset,
        )
        return (updated, None)

    high_final, total_final, accum_final = lax.scan(
        sweep_advance, initial, jnp.arange(piece_rows // step_rows, dtype=jnp.int32)
    )[0]
    attn_out = (
        (accum_final / jnp.moveaxis(total_final, -1, 0)[..., None])
        .reshape(1, local_rows, QHEADS * QDIM)
        .astype(jnp.bfloat16)
    )
    return (mixer_out, attn_out)


def solution(mesh):
    placed = (
        P("batch", "ctx", None),
        P("batch", "ctx", None),
        P("batch", "ctx", None),
        P(),
        P(),
        P(),
        P(),
        P(),
        P(),
        P("batch", "ctx", None),
        P("batch", "ctx", None),
        P("batch", "ctx", None),
    )
    return jax.shard_map(
        on_device,
        mesh=mesh,
        in_specs=placed,
        out_specs=(P("batch", "ctx", None), P("batch", "ctx", None)),
        check_vma=False,
    )
```

profile of v0, /device:TPU:27, one launch (start us, length us, event | category | flops | bytes accessed | tf_op | source)
XLA Modules:
  0.0 550.0 jit_solution(5243147945662274098)
XLA Ops:
  8.7 9.7 %all_to_all.108 = bf16[1,128,2,8,128]{1,4,2,0,3:T(8,128)(2,1)S(1)} all-to-all(bf16[1,128,2,8,128]{1,4,2,0,3:T(8,128)(2,1)S(1)} %copy.285), channel_id=1, replica_groups=mesh['ctx'=16,'batch'=2] {'batch'}, dimensions={3} | all-to-all | bytes 1048576 | tf_op jit(solution)/shard_map/all_to_all | solution.py:173
  22.5 3.3 all-to-all-start
  25.7 6.9 %copy.313 = bf16[1,128,8192]{1,0,2:T(2,128)(2,1)} copy(bf16[1,128,8192]{2,1,0:T(8,128)(2,1)S(1)} %slice-done) | data formatting | bytes 4194304
  32.7 45.2 %reduce.10 = bf16[8192,128]{1,0:T(8,128)(2,1)S(1)} reduce(bf16[8192,1,128]{2,1,0:T(2,128)(2,1)} %bitcast.255, bf16[]{:T(256)} %broadcast.358), dimensions={1}, to_apply=%bitcast.180.reduce_sub_computation | reduce | bytes 4194306
  79.5 3.8 all-to-all-start.2
  83.9 22.4 %all-to-all-done.2 = bf16[2,2,262144]{2,1,0:T(2,128)(2,1)S(1)} async-done(((bf16[2,2,262144]{2,1,0:T(2,128)(2,1)}), bf16[2,2,262144]{2,1,0:T(2,128)(2,1)S(1)}, u32[]{:S(2)}, u32[]{:S(2)}) %all-to-all-start.2) | async-done | bytes 2097184 | tf_op jit(solution)/shard_map/all_to_all | solution.py:156
  106.3 8.6 %all-to-all-start.1 = ((bf16[2,128,64]{1,0,2:T(2,128)(2,1)}), bf16[2,128,64]{1,0,2:T(2,128)(2,1)S(1)}, u32[]{:S(2)}, u32[]{:S(2)}) async-start(bf16[2,128,64]{1,0,2:T(2,128)(2,1)} %copy.277), calls=%async_computation.1 | async-start | bytes 65536 | tf_op jit(solution)/shard_map/all_to_all | solution.py:164
  114.9 3.1 reshape.502
  118.0 2.5 copy.312
  120.5 18.1 %copy.280 = bf16[2,128,4096]{1,0,2:T(2,128)(2,1)} copy(bf16[2,128,4096]{1,2,0:T(8,128)(2,1)S(1)} %bitcast.261) | data formatting | bytes 4194304 | tf_op jit(solution)/shard_map/all_to_all | solution.py:156
  138.7 6.0 %all-to-all-start.3 = ((bf16[2,128,4096]{1,0,2:T(2,128)(2,1)}), bf16[2,128,4096]{1,0,2:T(2,128)(2,1)S(1)}, u32[]{:S(2)}, u32[]{:S(2)}) async-start(bf16[2,128,4096]{1,0,2:T(2,128)(2,1)} %copy.280), calls=%async_computation.3 | async-start | bytes 4194304 | tf_op jit(solution)/shard_map/all_to_all | solution.py:155
  149.9 59.8 %all-to-all-done.3 = bf16[2,128,4096]{1,0,2:T(2,128)(2,1)S(1)} async-done(((bf16[2,128,4096]{1,0,2:T(2,128)(2,1)}), bf16[2,128,4096]{1,0,2:T(2,128)(2,1)S(1)}, u32[]{:S(2)}, u32[]{:S(2)}) %all-to-all-start.3) | async-done | bytes 2097184 | tf_op jit(solution)/shard_map/all_to_all | solution.py:155
  211.4 2.9 copy.282
  214.7 3.7 multiply_convert_fusion.4
  218.4 2.5 copy.283
  222.6 18.1 %copy.287 = bf16[2,1,2048,2,1,128]{5,3,2,0,4,1:T(2,128)(2,1)} copy(bf16[2,1,2048,2,1,128]{5,2,4,0,3,1:T(8,128)(2,1)S(1)} %constant_dynamic-slice_fusion.8) | data formatting | bytes 4194304 | tf_op jit(solution)/shard_map/dynamic_slice | solution.py:175
  240.7 3.2 reshape.473
  244.3 3.7 multiply_convert_fusion.3
  248.3 108.3 %while.32 = (s32[]{:T(128)}, f32[2,1,4,128,64]{3,4,2,0,1:T(8,128)S(1)}, s32[2]{0:T(128)S(1)}, bf16[16,2,128,1,4,64]{2,5,4,1,3,0:T(8,128)(2,1)}, s32[16]{0:T(128)...) while((s32[]{:T(128)}, ...), condition=%wide.region_4.5_spmd.clone, body=%wide.region_2.4_spmd.clone.sunk | while | flops 228152848 | bytes 3484125 | solution.py:110
  264.5 2.0 fusion.122
  305.1 2.1 fusion.122
  356.6 6.9 %copy.305 = bf16[2,16,128,1,4,64]{5,4,0,2,1,3:T(4,128)(2,1)} copy(bf16[2,16,128,1,4,64]{2,5,4,0,3,1:T(8,128)(2,1)} %bitcast.271) | data formatting | bytes 4194304 | tf_op jit(solution)/shard_map/convert_element_type | solution.py:235
  363.5 8.2 %reshape.497 = bf16[2,2048,256]{2,0,1:T(2,128)(2,1)} reshape(bf16[2,16,128,1,4,64]{5,4,0,2,1,3:T(4,128)(2,1)} %copy.305) | data formatting | bytes 4194304 | tf_op jit(solution)/shard_map/convert_element_type | solution.py:235
  371.8 6.1 %all-to-all-start.5 = ((bf16[2,2048,256]{2,0,1:T(2,128)(2,1)}), bf16[2,2048,256]{2,0,1:T(2,128)(2,1)S(1)}, u32[]{:S(2)}, u32[]{:S(2)}) async-start(bf16[2,2048,256]{2,0,1:T(2,128)(2,1)} %reshape.497), calls=%async_computation.5 | async-start | bytes 4194304 | tf_op jit(solution)/shard_map/all_to_all | solution.py:239
  381.4 42.9 %all-to-all-done.5 = bf16[2,2048,256]{2,0,1:T(2,128)(2,1)S(1)} async-done(((bf16[2,2048,256]{2,0,1:T(2,128)(2,1)}), bf16[2,2048,256]{2,0,1:T(2,128)(2,1)S(1)}, u32[]{:S(2)}, u32[]{:S(2)}) %all-to-all-start.5) | async-done | bytes 2097184 | tf_op jit(solution)/shard_map/all_to_all | solution.py:239
  425.8 3.9 copy.292
  429.8 4.8 all-to-all-start.6
  434.6 70.9 %while.33 = (s32[]{:T(128)}, f32[8,4,128]{2,1,0:T(4,128)S(1)}, f32[8,4,128]{2,1,0:T(4,128)S(1)}, f32[128,8,4,128]{0,3,2,1:T(8,128)}, s32[1,1,6]{2,1,0:T(1,128)S(...) while((s32[]{:T(128)}, f32[8,4,128]{2,1,0:T(4,128)S(1)}, ...), condition=%wide.region_13.14_spmd.clone, body=%wide.region_9.13_spmd.clone.sunk | while | flops 1103005312 | bytes 70795024 | solution.py:303
  437.9 4.7 fusion.129
  442.7 7.1 %bitcast_add_fusion.2 = f32[128,8,4,128]{0,3,2,1:T(8,128)} fusion(f32[128,8,4,128]{0,3,2,1:T(8,128)} %get-tuple-element.763, bf16[512,8,128,1]{0,2,3,1:T(8,128)(2,1)S(1)} %bitcast.254, f32[8,512,128,4]{2,1,3,0:T(8,128)} %get-tuple-element.694, f32[8,4,128]{2,1,0:T(4,128)S(1)} %get-tuple-element.776, pred[128,512]{0,1:T(8,128)(4,1)S(1)} %fusion.128, ...), kind=kOutput, calls=%fused_computation.8.clone.1 | convolution fusion | flops 548929536 | bytes 13729793 | tf_op jit(solution)/shard_map/while/body/eval_jaxpr/kgqr,rkd->qkgd/dot_general | solution.py:275
  449.8 2.1 fusion.131
  455.2 4.7 fusion.129
  459.9 7.7 %bitcast_add_fusion.2 = f32[128,8,4,128]{0,3,2,1:T(8,128)} fusion(f32[128,8,4,128]{0,3,2,1:T(8,128)} %get-tuple-element.763, bf16[512,8,128,1]{0,2,3,1:T(8,128)(2,1)S(1)} %bitcast.254, f32[8,512,128,4]{2,1,3,0:T(8,128)} %get-tuple-element.694, f32[8,4,128]{2,1,0:T(4,128)S(1)} %get-tuple-element.776, pred[128,512]{0,1:T(8,128)(4,1)S(1)} %fusion.128, ...), kind=kOutput, calls=%fused_computation.8.clone.1 | convolution fusion | flops 548929536 | bytes 13729793 | tf_op jit(solution)/shard_map/while/body/eval_jaxpr/kgqr,rkd->qkgd/dot_general | solution.py:275
  467.6 2.1 fusion.131
  473.1 4.7 fusion.129
  477.8 7.7 %bitcast_add_fusion.2 = f32[128,8,4,128]{0,3,2,1:T(8,128)} fusion(f32[128,8,4,128]{0,3,2,1:T(8,128)} %get-tuple-element.763, bf16[512,8,128,1]{0,2,3,1:T(8,128)(2,1)S(1)} %bitcast.254, f32[8,512,128,4]{2,1,3,0:T(8,128)} %get-tuple-element.694, f32[8,4,128]{2,1,0:T(4,128)S(1)} %get-tuple-element.776, pred[128,512]{0,1:T(8,128)(4,1)S(1)} %fusion.128, ...), kind=kOutput, calls=%fused_computation.8.clone.1 | convolution fusion | flops 548929536 | bytes 13729793 | tf_op jit(solution)/shard_map/while/body/eval_jaxpr/kgqr,rkd->qkgd/dot_general | solution.py:275
  485.5 2.1 fusion.131
  491.0 4.7 fusion.129
  495.7 7.7 %bitcast_add_fusion.2 = f32[128,8,4,128]{0,3,2,1:T(8,128)} fusion(f32[128,8,4,128]{0,3,2,1:T(8,128)} %get-tuple-element.763, bf16[512,8,128,1]{0,2,3,1:T(8,128)(2,1)S(1)} %bitcast.254, f32[8,512,128,4]{2,1,3,0:T(8,128)} %get-tuple-element.694, f32[8,4,128]{2,1,0:T(4,128)S(1)} %get-tuple-element.776, pred[128,512]{0,1:T(8,128)(4,1)S(1)} %fusion.128, ...), kind=kOutput, calls=%fused_computation.8.clone.1 | convolution fusion | flops 548929536 | bytes 13729793 | tf_op jit(solution)/shard_map/while/body/eval_jaxpr/kgqr,rkd->qkgd/dot_general | solution.py:275
  503.4 2.1 fusion.131
  508.7 3.8 bitcast_convert_fusion
  512.6 5.8 %copy.293 = f32[1,128,8192]{2,1,0:T(8,128)} copy(f32[1,128,8192]{1,2,0:T(8,128)} %bitcast.258) | data formatting | bytes 8388608 | tf_op jit(solution)/shard_map/convert_element_type | solution.py:117
  518.4 3.3 fusion.79
  521.7 5.2 copy.316
  526.9 2.5 reduce_sum.49
  529.5 2.3 mul.305
  531.9 5.0 mul.306
  536.8 6.2 %multiply_convert_fusion.2 = bf16[1,128,8192]{2,1,0:T(8,128)(2,1)} fusion(f32[1,128,8192]{2,1,0:T(8,128)} %mul.306, f32[8192]{0:T(1024)S(1)} %copy-done.5, f32[1,128,8192]{2,1,0:T(8,128)} %copy.293, bf16[1,128,8192]{2,1,0:T(8,128)(2,1)S(1)} %copy-done.1), kind=kLoop, calls=%fused_computation.106 | loop fusion | flops 9437184 | bytes 12615680 | tf_op jit(solution)/shard_map/convert_element_type | solution.py:120
  (538 shorter events, 128.2 us)
Async XLA Ops:
  7.2 12.3 %copy-start.3 = (bf16[1,128,1024]{2,1,0:T(8,128)(2,1)S(1)}, bf16[1,128,1024]{2,1,0:T(8,128)(2,1)}, u32[]{:S(2)}) copy-start(bf16[1,128,1024]{2,1,0:T(8,128)(2,1)} %param.26) | copy-start | bytes 786436
  7.2 13.2 %copy-start.6 = (bf16[1,128,128]{2,1,0:T(8,128)(2,1)S(1)}, bf16[1,128,128]{2,1,0:T(8,128)(2,1)}, u32[]{:S(2)}) copy-start(bf16[1,128,128]{2,1,0:T(8,128)(2,1)} %param.18) | copy-start | bytes 98308
  7.2 213.7 %all-gather.7.cloned.1.call-start = ((), (), s32[]{:S(2)}) async-start(), calls=%async_computation.7 | async-start | bytes 8912896 | tf_op jit(solution)/shard_map/all_gather | solution.py:174
  8.7 17.1 %slice-start = ((bf16[1,128,10240]{2,1,0:T(8,128)(2,1)}), bf16[1,128,8192]{2,1,0:T(8,128)(2,1)S(1)}, s32[]{:S(2)}) async-start(bf16[1,128,10240]{2,1,0:T(8,128)(2,1)} %param.16), calls=%async_computation.10 | async-start | bytes 4194304 | tf_op jit(solution)/shard_map/slice | solution.py:157
  19.4 415.2 %all-gather.9.cloned.1.call-start = ((), (), s32[]{:S(2)}) async-start(), calls=%async_computation.8 | async-start | bytes 4456448 | tf_op jit(solution)/shard_map/all_gather | solution.py:288
  22.5 57.0 %all-to-all-start = ((bf16[2,2,4096]{2,1,0:T(2,128)(2,1)}), bf16[2,2,4096]{2,1,0:T(2,128)(2,1)S(1)}, u32[]{:S(2)}, u32[]{:S(2)}) async-start(bf16[2,2,4096]{2,1,0:T(2,128)(2,1)} %reshape.499), calls=%async_computation | async-start | bytes 65536 | tf_op jit(solution)/shard_map/all_to_all | solution.py:165
  79.5 26.9 %all-to-all-start.2 = ((bf16[2,2,262144]{2,1,0:T(2,128)(2,1)}), bf16[2,2,262144]{2,1,0:T(2,128)(2,1)S(1)}, u32[]{:S(2)}, u32[]{:S(2)}) async-start(bf16[2,2,262144]{2,1,0:T(2,128)(2,1)} %reshape.501), calls=%async_computation.2 | async-start | bytes 4194304 | tf_op jit(solution)/shard_map/all_to_all | solution.py:156
  106.3 32.3 %all-to-all-start.1 = ((bf16[2,128,64]{1,0,2:T(2,128)(2,1)}), bf16[2,128,64]{1,0,2:T(2,128)(2,1)S(1)}, u32[]{:S(2)}, u32[]{:S(2)}) async-start(bf16[2,128,64]{1,0,2:T(2,128)(2,1)} %copy.277), calls=%async_computation.1 | async-start | bytes 65536 | tf_op jit(solution)/shard_map/all_to_all | solution.py:164
  120.5 24.5 %copy-start.4 = (bf16[1,128,1024]{2,1,0:T(8,128)(2,1)S(1)}, bf16[1,128,1024]{2,1,0:T(8,128)(2,1)}, u32[]{:S(2)}) copy-start(bf16[1,128,1024]{2,1,0:T(8,128)(2,1)} %param.27) | copy-start | bytes 786436
  120.5 25.4 %copy-start.7 = (s32[2,6]{1,0:T(2,128)S(1)}, s32[2,6]{1,0:T(2,128)}, u32[]{:S(2)}) copy-start(s32[2,6]{1,0:T(2,128)} %param.24) | copy-start | bytes 148
  120.5 25.7 %copy-start.8 = (f32[128]{0:T(128)S(1)}, f32[128]{0:T(128)}, u32[]{:S(2)}) copy-start(f32[128]{0:T(128)} %param.21) | copy-start | bytes 1540
  120.5 25.7 %copy-start.9 = (f32[128]{0:T(128)S(1)}, f32[128]{0:T(128)}, u32[]{:S(2)}) copy-start(f32[128]{0:T(128)} %param.22) | copy-start | bytes 1540
  138.7 71.1 %all-to-all-start.3 = ((bf16[2,128,4096]{1,0,2:T(2,128)(2,1)}), bf16[2,128,4096]{1,0,2:T(2,128)(2,1)S(1)}, u32[]{:S(2)}, u32[]{:S(2)}) async-start(bf16[2,128,4096]{1,0,2:T(2,128)(2,1)} %copy.280), calls=%async_computation.3 | async-start | bytes 4194304 | tf_op jit(solution)/shard_map/all_to_all | solution.py:155
  144.7 289.9 %all-gather.11.cloned.1.call-start = ((), (), s32[]{:S(2)}) async-start(), calls=%async_computation.9 | async-start | bytes 4456448 | tf_op jit(solution)/shard_map/all_gather | solution.py:289
  363.5 14.8 %copy-start.2 = (bf16[1,128,4096]{2,1,0:T(8,128)(2,1)S(1)}, bf16[1,128,4096]{2,1,0:T(8,128)(2,1)}, u32[]{:S(2)}) copy-start(bf16[1,128,4096]{2,1,0:T(8,128)(2,1)} %param.25) | copy-start | bytes 3145732
  371.8 52.5 %all-to-all-start.5 = ((bf16[2,2048,256]{2,0,1:T(2,128)(2,1)}), bf16[2,2048,256]{2,0,1:T(2,128)(2,1)S(1)}, u32[]{:S(2)}, u32[]{:S(2)}) async-start(bf16[2,2048,256]{2,0,1:T(2,128)(2,1)} %reshape.497), calls=%async_computation.5 | async-start | bytes 4194304 | tf_op jit(solution)/shard_map/all_to_all | solution.py:239
  429.8 79.0 %all-to-all-start.6 = ((bf16[2,128,4096]{1,2,0:T(8,128)(2,1)}), bf16[2,128,4096]{1,2,0:T(8,128)(2,1)}, u32[]{:S(2)}, u32[]{:S(2)}) async-start(bf16[2,128,4096]{1,2,0:T(8,128)(2,1)} %bitcast.29), calls=%async_computation.6 | async-start | bytes 4194304 | tf_op jit(solution)/shard_map/all_to_all | solution.py:238
  442.6 7.1 %copy-start = (f32[8,512,128,4]{2,1,3,0:T(8,128)S(1)}, f32[8,512,128,4]{2,1,3,0:T(8,128)}, u32[]{:S(2)}) copy-start(f32[8,512,128,4]{2,1,3,0:T(8,128)} %get-tuple-element.694) | copy-start | bytes 25165828 | tf_op jit(solution)/shard_map/while
  459.9 7.7 %copy-start = (f32[8,512,128,4]{2,1,3,0:T(8,128)S(1)}, f32[8,512,128,4]{2,1,3,0:T(8,128)}, u32[]{:S(2)}) copy-start(f32[8,512,128,4]{2,1,3,0:T(8,128)} %get-tuple-element.694) | copy-start | bytes 25165828 | tf_op jit(solution)/shard_map/while
  477.8 7.7 %copy-start = (f32[8,512,128,4]{2,1,3,0:T(8,128)S(1)}, f32[8,512,128,4]{2,1,3,0:T(8,128)}, u32[]{:S(2)}) copy-start(f32[8,512,128,4]{2,1,3,0:T(8,128)} %get-tuple-element.694) | copy-start | bytes 25165828 | tf_op jit(solution)/shard_map/while
  495.7 7.7 %copy-start = (f32[8,512,128,4]{2,1,3,0:T(8,128)S(1)}, f32[8,512,128,4]{2,1,3,0:T(8,128)}, u32[]{:S(2)}) copy-start(f32[8,512,128,4]{2,1,3,0:T(8,128)} %get-tuple-element.694) | copy-start | bytes 25165828 | tf_op jit(solution)/shard_map/while
  512.6 5.8 %copy-start.1 = (bf16[1,128,8192]{2,1,0:T(8,128)(2,1)S(1)}, bf16[1,128,8192]{2,1,0:T(8,128)(2,1)}, u32[]{:S(2)}) copy-start(bf16[1,128,8192]{2,1,0:T(8,128)(2,1)} %param.17) | copy-start | bytes 6291460
  531.9 5.0 copy-start.5
Sparse Core Ops, SparseCore 0:
  19.6 73.8 all-gather.6
  95.6 51.5 all-gather.8
  149.4 72.6 all-gather.10
where the time goes:
time: 559 us; the launch traced here: 550 us
  local copies, waits for them, and re-layouts  145 us (26%)
  waiting for transfers between devices  125 us (22%)
  matrix products  107 us (19%)
  other arithmetic  99.9 us (18%)
  starting transfers between devices  32.9 us (6%)
  loops' own time  15.3 us (3%)
  between operations  14.7 us (3%)
  blocking collectives  9.72 us (2%)
    all_to_all x1, waiting for transfers between devices, on_device(): lax.all_to_all(lax.all_to_all(mixer_input[:, :, :inner_width], 'batch', s...  59.8 us
    unnamed x6, other arithmetic  46 us
    all_to_all x1, waiting for transfers between devices, on_device(): lax.all_to_all(mixed_send, 'ctx', split_axis=1, concat_axis=2, tiled=True)  42.9 us
    dot_general x16, matrix products, ssd_block(): jnp.einsum('sqkgr,skgrp->sqgrp', weights, head_inputs, preferred_element_...  32.4 us
    dot_general x4, matrix products, attend_rows(): jnp.einsum('kgqr,rkd->qkgd', numerators.astype(jnp.bfloat16), value_rows....  30.2 us
    unnamed x33, local copies, waits for them, and re-layouts  25.6 us
    all_to_all x1, waiting for transfers between devices, on_device(): lax.all_to_all(mixer_input[:, :, :inner_width], 'batch', split_axis=2, co...  22.4 us
    dynamic_slice x2, local copies, waits for them, and re-layouts, on_device(): lax.dynamic_slice_in_dim(whole_proj, group_local, 1, 3)  19.9 us
  transfers between devices with their start and end apart: 9, of which 3 were waited for; matrix products, arithmetic and copies ran while one was open for 57% of the time, Pallas kernels for 0%

commit v1 on v0

v1 whole, which is shorter than its diff:
```python
import functools

import jax
import jax.numpy as jnp
from jax import lax
from jax.experimental import pallas as pl
from jax.experimental.pallas import tpu as pltpu
from jax.sharding import PartitionSpec as P

HEADS = 128
HEAD_DIM = 64
STATE = 128
GROUPS = 8
QHEADS = 32
KVHEADS = 8
QDIM = 128
PER_GROUP = HEADS // GROUPS
GROUP_WIDTH = PER_GROUP * HEAD_DIM
RIM = 16

EPSILON = 1e-05
NEGATIVE = -1e30
F32 = jnp.float32
BF16 = jnp.bfloat16
MESH = pl.DeviceIdType.MESH


def start_of(info_ref, positions, docs):
    start = jnp.zeros_like(positions)
    for doc in range(1, docs):
        first = info_ref[1 + doc]
        start = jnp.where(positions >= first, first, start)
    return start


def log_decays(step_ref, rate_ref, rows):
    steps = jax.nn.softplus(step_ref[...].astype(F32))
    fall = -steps * rate_ref[...]
    lower = (
        lax.broadcasted_iota(jnp.int32, (rows, rows), 0)
        >= lax.broadcasted_iota(jnp.int32, (rows, rows), 1)
    ).astype(F32)
    return steps, jnp.dot(
        lower, fall, precision=lax.Precision.HIGHEST, preferred_element_type=F32
    )


def spread_heads(per_head):
    high = per_head.astype(BF16)
    low = (per_head - high.astype(F32)).astype(BF16)
    both = jnp.concatenate([high, low], axis=1)
    row = lax.broadcasted_iota(jnp.int32, (2 * PER_GROUP, GROUP_WIDTH), 0)
    col = lax.broadcasted_iota(jnp.int32, (2 * PER_GROUP, GROUP_WIDTH), 1)
    own = (lax.rem(row, PER_GROUP) == lax.div(col, HEAD_DIM)).astype(BF16)
    return jnp.dot(both, own, preferred_element_type=F32)


def conv_silu(in_ref, rim_ref, weight_ref, bias_ref, pad_ref, same):
    rows, width = in_ref.shape
    pad_ref[0:8, 0:width] = rim_ref[8:16, :].astype(F32)
    pad_ref[8 : 8 + rows, 0:width] = in_ref[...].astype(F32)
    taps = weight_ref.shape[0]
    summed = pad_ref[8 : 8 + rows, 0:width] * weight_ref[taps - 1 : taps, :] + bias_ref[...]
    for back in range(1, taps):
        window = pad_ref[8 - back : 8 - back + rows, 0:width]
        tap = weight_ref[taps - 1 - back : taps - back, :]
        summed = summed + jnp.where(same[back - 1], window * tap, 0.0)
    return (summed * jax.nn.sigmoid(summed)).astype(BF16)


def fresh_kernel(
    docs,
    info_ref,
    x_ref, b_ref, c_ref,
    rim_x_ref, rim_b_ref, rim_c_ref,
    w_x_ref, w_b_ref, w_c_ref,
    o_x_ref, o_b_ref, o_c_ref,
    step_ref, rate_ref,
    act_ref, proj_ref, fresh_ref, through_ref,
    pad_ref, trail_ref, last_ref,
):
    rows = x_ref.shape[0]
    group = pl.program_id(0)
    base = info_ref[0]
    pos = base + lax.broadcasted_iota(jnp.int32, (rows, 1), 0)
    start = start_of(info_ref, pos, docs)

    @pl.when(group == 0)
    def _():
        steps, decay = log_decays(step_ref, rate_ref, rows)
        last_pos = jnp.full((rows, 1), base + rows - 1, jnp.int32)
        last_start = start_of(info_ref, last_pos, docs)
        final = decay[rows - 1 : rows, :]
        trail = jnp.where(pos >= last_start, jnp.exp(final - decay) * steps, 0.0)
        carry = jnp.where(
            last_start[0:8] < base, jnp.exp(jnp.broadcast_to(final, (8, HEADS))), 0.0
        )
        for k in range(GROUPS):
            trail_ref[k] = trail[:, k * PER_GROUP : (k + 1) * PER_GROUP]
            last_ref[k] = carry[:, k * PER_GROUP : (k + 1) * PER_GROUP]

    same = [pos - back >= start for back in range(1, w_x_ref.shape[0])]
    x = conv_silu(x_ref, rim_x_ref, w_x_ref, o_x_ref, pad_ref, same)
    b = conv_silu(b_ref, rim_b_ref, w_b_ref, o_b_ref, pad_ref, same)
    c = conv_silu(c_ref, rim_c_ref, w_c_ref, o_c_ref, pad_ref, same)
    act_ref[...] = x
    proj_ref[0, 0] = b
    proj_ref[0, 1] = c
    scaled = (x.astype(F32) * spread_heads(trail_ref[group])).astype(BF16)
    fresh_ref[0] = lax.dot_general(
        b, scaled, (((0,), (0,)), ((), ())), preferred_element_type=F32
    ).astype(BF16)
    through_ref[0] = spread_heads(last_ref[group])


def chain_kernel(n, fresh_ref, through_ref, before_ref, got, sent, send_sem, recv_sem):
    rank = lax.axis_index("ctx")
    right, left = lax.rem(rank + 1, n), lax.rem(rank + n - 1, n)
    barrier = pltpu.get_barrier_semaphore()
    for neighbour in (left, right):
        pl.semaphore_signal(barrier, inc=1, device_id={"ctx": neighbour}, device_id_type=MESH)
    pl.semaphore_wait(barrier, 2)
    pieces = got.shape[0]
    splits = pieces // GROUPS
    width = got.shape[2]

    def hand_on(piece):
        return pltpu.make_async_remote_copy(
            src_ref=sent.at[piece],
            dst_ref=got.at[piece],
            send_sem=send_sem.at[piece],
            recv_sem=recv_sem.at[piece],
            device_id={"ctx": right},
            device_id_type=MESH,
        )

    @pl.when(rank == 0)
    def _():
        for piece in range(pieces):
            cols = slice((piece % splits) * width, (piece % splits + 1) * width)
            sent[piece] = fresh_ref[piece // splits, :, cols]
            hand_on(piece).start()
        before_ref[...] = jnp.zeros_like(before_ref)

    @pl.when(rank > 0)
    def _():
        for piece in range(pieces):
            group, cols = piece // splits, slice(
                (piece % splits) * width, (piece % splits + 1) * width
            )
            hand_on(piece).wait_recv()

            @pl.when(rank < n - 1)
            def _():
                sent[piece] = (
                    through_ref[group, 0:1, cols] * got[piece].astype(F32)
                    + fresh_ref[group, :, cols].astype(F32)
                ).astype(BF16)
                hand_on(piece).start()

            before_ref[group, :, cols] = got[piece]

    @pl.when(rank < n - 1)
    def _():
        for piece in range(pieces):
            hand_on(piece).wait_send()


def mix_kernel(
    docs,
    info_ref,
    x_ref, proj_ref, before_ref, z_ref, gain_ref, skip_ref, step_ref, rate_ref,
    out_ref,
    decay_ref, late_ref, row_ref,
):
    rows = x_ref.shape[0]
    group = pl.program_id(0)
    base = info_ref[0]
    pos = base + lax.broadcasted_iota(jnp.int32, (rows, 1), 0)
    start = start_of(info_ref, pos, docs)

    @pl.when(group == 0)
    def _():
        steps, decay = log_decays(step_ref, rate_ref, rows)
        late = jnp.where(start < base, jnp.exp(decay), 0.0)
        for k in range(GROUPS):
            decay_ref[k] = decay[:, k * PER_GROUP : (k + 1) * PER_GROUP]
            late_ref[k] = late[:, k * PER_GROUP : (k + 1) * PER_GROUP]
        row_ref[...] = (decay - jnp.log(steps)).T

    x = x_ref[...]
    b, c = proj_ref[0, 0], proj_ref[0, 1]
    key_pos = base + lax.broadcasted_iota(jnp.int32, (rows, rows), 1)
    related = (key_pos <= pos) & (key_pos >= start)
    scores = lax.dot_general(c, b, (((1,), (1,)), ((), ())), preferred_element_type=F32)
    scores = jnp.where(related, scores, 0.0)
    columns = decay_ref[group]
    lines = row_ref[pl.ds(pl.multiple_of(group * PER_GROUP, PER_GROUP), PER_GROUP), :]
    lane = lax.broadcasted_iota(jnp.int32, (rows, 2 * HEAD_DIM), 1)
    first = lane < HEAD_DIM
    parts = []
    for pair in range(PER_GROUP // 2):
        weights = []
        for head in (2 * pair, 2 * pair + 1):
            weights.append(
                (
                    scores * jnp.exp(columns[:, head : head + 1] - lines[head : head + 1, :])
                ).astype(BF16)
            )
        own = x[:, pair * 2 * HEAD_DIM : (pair + 1) * 2 * HEAD_DIM]
        zero = jnp.zeros_like(own)
        stacked = jnp.concatenate([jnp.where(first, own, zero), jnp.where(first, zero, own)], axis=0)
        parts.append(
            jnp.dot(jnp.concatenate(weights, axis=1), stacked, preferred_element_type=F32)
        )
    inner = jnp.concatenate(parts, axis=1)
    carried = jnp.dot(c, before_ref[0], preferred_element_type=F32)
    mixed = inner + carried * spread_heads(late_ref[group]) + skip_ref[...] * x.astype(F32)
    z = z_ref[...].astype(F32)
    gated = mixed * (z * jax.nn.sigmoid(z))
    scaling = lax.rsqrt(jnp.mean(gated * gated, axis=1, keepdims=True) + EPSILON)
    out_ref[...] = (gated * scaling * gain_ref[...]).astype(BF16)


def attend_kernel(docs, step_rows, info_ref, q_ref, k_ref, v_ref, out_ref):
    rows = q_ref.shape[0]
    group_size = q_ref.shape[1] // QDIM
    base = info_ref[0]
    q = jnp.concatenate([q_ref[:, i * QDIM : (i + 1) * QDIM] for i in range(group_size)], axis=0)
    tall = rows * group_size
    pos = base + lax.rem(lax.broadcasted_iota(jnp.int32, (tall, 1), 0), rows)
    start = start_of(info_ref, pos, docs)
    earliest = jnp.int32(0)
    for doc in range(1, docs):
        earliest = jnp.where(base >= info_ref[1 + doc], info_ref[1 + doc], earliest)
    scaling = QDIM ** (-0.5)

    def step(block, carry):
        high, accum = carry
        offset = pl.multiple_of(block * step_rows, step_rows)
        keys = k_ref[pl.ds(offset, step_rows), :]
        values = v_ref[pl.ds(offset, step_rows), :]
        scores = (
            lax.dot_general(q, keys, (((1,), (1,)), ((), ())), preferred_element_type=F32)
            * scaling
        )
        key_pos = offset + lax.broadcasted_iota(jnp.int32, (tall, step_rows), 1)
        visible = (key_pos <= pos) & (key_pos >= start)
        masked = jnp.where(visible, scores, NEGATIVE)
        high_next = jnp.maximum(high, jnp.max(masked, axis=1, keepdims=True))
        numerators = jnp.where(visible, jnp.exp(masked - high_next), 0.0)
        fading = jnp.exp(high - high_next)
        wide = jnp.concatenate([values, jnp.ones_like(values)], axis=1)
        accum_next = accum * fading + jnp.dot(
            numerators.astype(BF16), wide, preferred_element_type=F32
        )
        return high_next, accum_next

    first_block = lax.div(earliest, step_rows)
    last_block = lax.div(base + rows - 1, step_rows) + 1
    high, accum = lax.fori_loop(
        first_block,
        last_block,
        step,
        (jnp.full((tall, 1), NEGATIVE, F32), jnp.zeros((tall, 2 * QDIM), F32)),
    )
    result = (accum[:, :QDIM] / accum[:, QDIM:]).astype(BF16)
    for i in range(group_size):
        out_ref[:, i * QDIM : (i + 1) * QDIM] = result[i * rows : (i + 1) * rows, :]


def params(limit, **more):
    return pltpu.CompilerParams(vmem_limit_bytes=limit * 2**20, **more)


def on_device(
    mixer_input,
    z_gate,
    time_step,
    conv_weight,
    conv_bias,
    decay_rate,
    skip_gain,
    norm_gain,
    doc_lengths,
    queries,
    attn_keys,
    attn_values,
):
    rows = mixer_input.shape[1]
    width = mixer_input.shape[2]
    inner_width = HEADS * HEAD_DIM
    docs = doc_lengths.shape[1]
    taps = conv_weight.shape[0]
    n = lax.axis_size("ctx")
    rank = lax.axis_index("ctx")
    keys = lax.all_gather(attn_keys[0], "ctx", axis=0, tiled=True)
    values = lax.all_gather(attn_values[0], "ctx", axis=0, tiled=True)
    rim = lax.ppermute(
        mixer_input[0, rows - RIM :, :], "ctx", [(i, i + 1) for i in range(n - 1)]
    )
    lengths = lax.dynamic_slice_in_dim(doc_lengths, lax.axis_index("batch"), 1, 0)[0]
    info = jnp.concatenate([(rank * rows).astype(jnp.int32)[None], jnp.cumsum(lengths) - lengths])
    rates = decay_rate[None]
    bias = conv_bias[None]
    skips = jnp.repeat(skip_gain, HEAD_DIM)[None]
    first_b = inner_width // STATE
    first_c = first_b + GROUPS
    smem = pl.BlockSpec(memory_space=pltpu.SMEM)

    def wide(height):
        return pl.BlockSpec((height, GROUP_WIDTH), lambda g: (0, g))

    def narrow(height, first):
        return pl.BlockSpec((height, STATE), lambda g: (0, first + g))

    def trio(height):
        return [wide(height), narrow(height, first_b), narrow(height, first_c)]

    whole = pl.BlockSpec((rows, HEADS), lambda g: (0, 0))
    rate_spec = pl.BlockSpec((1, HEADS), lambda g: (0, 0))
    per_group = lambda *shape: pl.BlockSpec((1,) + shape, lambda g: (g,) + (0,) * len(shape))
    inputs = mixer_input[0]
    act, proj, fresh, through = pl.pallas_call(
        functools.partial(fresh_kernel, docs),
        grid=(GROUPS,),
        in_specs=[smem] + trio(rows) + trio(RIM) + trio(taps) + trio(1) + [whole, rate_spec],
        out_specs=[
            wide(rows),
            per_group(2, rows, STATE),
            per_group(STATE, GROUP_WIDTH),
            per_group(8, GROUP_WIDTH),
        ],
        out_shape=[
            jax.ShapeDtypeStruct((rows, inner_width), BF16),
            jax.ShapeDtypeStruct((GROUPS, 2, rows, STATE), BF16),
            jax.ShapeDtypeStruct((GROUPS, STATE, GROUP_WIDTH), BF16),
            jax.ShapeDtypeStruct((GROUPS, 8, GROUP_WIDTH), F32),
        ],
        scratch_shapes=[
            pltpu.VMEM((8 + rows, GROUP_WIDTH), F32),
            pltpu.VMEM((GROUPS, rows, PER_GROUP), F32),
            pltpu.VMEM((GROUPS, 8, PER_GROUP), F32),
        ],
        compiler_params=params(24),
        cost_estimate=pl.CostEstimate(
            flops=6 * 10**8, bytes_accessed=8 * 10**6, transcendentals=10**6
        ),
        name="fresh_states",
    )(
        info,
        inputs, inputs, inputs,
        rim, rim, rim,
        conv_weight, conv_weight, conv_weight,
        bias, bias, bias,
        time_step[0],
        rates,
    )

    pieces = 2 * GROUPS
    piece_width = GROUPS * GROUP_WIDTH // pieces
    vmem = pl.BlockSpec(memory_space=pltpu.VMEM)
    before = pl.pallas_call(
        functools.partial(chain_kernel, n),
        in_specs=[vmem, vmem],
        out_specs=vmem,
        out_shape=jax.ShapeDtypeStruct((GROUPS, STATE, GROUP_WIDTH), BF16),
        scratch_shapes=[
            pltpu.VMEM((pieces, STATE, piece_width), BF16),
            pltpu.VMEM((pieces, STATE, piece_width), BF16),
            pltpu.SemaphoreType.DMA((pieces,)),
            pltpu.SemaphoreType.DMA((pieces,)),
        ],
        compiler_params=params(24, collective_id=0, has_side_effects=True),
        cost_estimate=pl.CostEstimate(
            flops=10**7, bytes_accessed=2 * 10**8, transcendentals=0
        ),
        name="hand_on_states",
    )(fresh, through)

    mixer_out = pl.pallas_call(
        functools.partial(mix_kernel, docs),
        grid=(GROUPS,),
        in_specs=[
            smem,
            wide(rows),
            per_group(2, rows, STATE),
            per_group(STATE, GROUP_WIDTH),
            wide(rows),
            wide(1),
            wide(1),
            whole,
            rate_spec,
        ],
        out_specs=wide(rows),
        out_shape=jax.ShapeDtypeStruct((rows, inner_width), BF16),
        scratch_shapes=[
            pltpu.VMEM((GROUPS, rows, PER_GROUP), F32),
            pltpu.VMEM((GROUPS, rows, PER_GROUP), F32),
            pltpu.VMEM((HEADS, rows), F32),
        ],
        compiler_params=params(24),
        cost_estimate=pl.CostEstimate(
            flops=10**9, bytes_accessed=10**7, transcendentals=4 * 10**6
        ),
        name="mix_heads",
    )(info, act, proj, before, z_gate[0], norm_gain[None], skips, time_step[0], rates)

    seq_len = keys.shape[0]
    q_width = queries.shape[2] // KVHEADS
    step_rows = 256
    attn_out = pl.pallas_call(
        functools.partial(attend_kernel, docs, step_rows),
        grid=(KVHEADS,),
        in_specs=[
            smem,
            pl.BlockSpec((rows, q_width), lambda g: (0, g)),
            pl.BlockSpec((seq_len, QDIM), lambda g: (0, g)),
            pl.BlockSpec((seq_len, QDIM), lambda g: (0, g)),
        ],
        out_specs=pl.BlockSpec((rows, q_width), lambda g: (0, g)),
        out_shape=jax.ShapeDtypeStruct((rows, QHEADS * QDIM), BF16),
        compiler_params=params(24),
        cost_estimate=pl.CostEstimate(
            flops=4 * 10**9, bytes_accessed=10**7, transcendentals=8 * 10**6
        ),
        name="attend",
    )(info, queries[0], keys, values)
    return (mixer_out[None], attn_out[None])


def solution(mesh):
    spread = P("batch", "ctx", None)
    placed = (spread,) * 3 + (P(),) * 6 + (spread,) * 3
    return jax.shard_map(
        on_device,
        mesh=mesh,
        in_specs=placed,
        out_specs=(spread, spread),
        check_vma=False,
    )
```

time: 559 us -> 189 us (0.34); the launches traced: 550 us -> 189 us
  Pallas kernels: 0 us -> 160 us
  local copies, waits for them, and re-layouts: 145 us -> 11.8 us
  waiting for transfers between devices: 125 us -> 1.38 us
  matrix products: 107 us -> 0 us
  other arithmetic: 99.9 us -> 0.95 us
  starting transfers between devices: 32.9 us -> 1.37 us
  loops' own time: 15.3 us -> 0 us
  blocking collectives: 9.72 us -> 0 us
    pallas_call x0 -> x4, Pallas kernels: none -> 160 us  [the longest x1 102 us: on_device(): pl.pallas_call(functools.partial(chain_kernel, n), in_specs=[vmem, vmem],...]
    all_to_all x6 -> x0, waiting for transfers between devices: 125 us -> none  [the longest x1 59.8 us: on_device(): lax.all_to_all(lax.all_to_all(mixer_input[:, :, :inner_width], 'batch', s...]
    dot_general x56 -> x0, matrix products: 103 us -> none  [the longest x16 32.4 us: ssd_block(): jnp.einsum('sqkgr,skgrp->sqgrp', weights, head_inputs, preferred_element_...]
    unnamed x6 -> x0, other arithmetic: 46 us -> none
    dynamic_slice x64 -> x0, local copies, waits for them, and re-layouts: 43 us -> none  [the longest x2 19.9 us: on_device(): lax.dynamic_slice_in_dim(whole_proj, group_local, 1, 3)]
    all_to_all x6 -> x0, starting transfers between devices: 32.5 us -> none  [the longest x1 8.59 us: on_device(): lax.all_to_all(lax.all_to_all(time_step, 'batch', split_axis=2, concat_ax...]
    all_to_all x8 -> x0, local copies, waits for them, and re-layouts: 29.9 us -> none  [the longest x1 18.1 us: on_device(): lax.all_to_all(mixer_input[:, :, :inner_width], 'batch', split_axis=2, co...]
    convert_element_type x5 -> x0, local copies, waits for them, and re-layouts: 24.7 us -> none  [the longest x2 15.2 us: on_device(): mixed_heads.astype(jnp.bfloat16)]
  transfers between devices with their start and end apart: 9 -> 3, of which waited for: 3 -> 0; matrix products, arithmetic and copies ran while one was open for 57% -> 2% of each run, Pallas kernels for 0% -> 64%
where the time goes in v1:
time: 189 us
  Pallas kernels  160 us (85%)
  between operations  14.1 us (7%)
  local copies, waits for them, and re-layouts  11.8 us (6%)
    pallas_call x1, Pallas kernels, on_device(): pl.pallas_call(functools.partial(chain_kernel, n), in_specs=[vmem, vmem],...  102 us
    pallas_call x1, Pallas kernels, on_device(): pl.pallas_call(functools.partial(attend_kernel, docs, step_rows), grid=(K...  38.8 us
    pallas_call x1, Pallas kernels, on_device(): pl.pallas_call(functools.partial(mix_kernel, docs), grid=(GROUPS,), in_sp...  10.2 us
    unnamed x22, local copies, waits for them, and re-layouts  9.24 us
    pallas_call x1, Pallas kernels, on_device(): pl.pallas_call(functools.partial(fresh_kernel, docs), grid=(GROUPS,), in_...  9.19 us
  transfers between devices with their start and end apart: 3, of which 0 were waited for; matrix products, arithmetic and copies ran while one was open for 2% of the time, Pallas kernels for 64%

profile of v1, /device:TPU:27, one launch (start us, length us, event | category | flops | bytes accessed | tf_op | source)
XLA Modules:
  0.0 189.3 jit_solution(17209469203784517773)
XLA Ops:
  7.2 0.0 all-gather.5.cloned.1.call-start
  7.2 0.7 all-gather.5.cloned.1.call-update
  7.9 0.0 all-gather.7.cloned.1.call-start
  7.9 0.7 all-gather.7.cloned.1.call-update
  8.6 1.0 slice_bitcast_fusion
  9.6 1.3 collective-permute-start
  11.0 0.7 fusion
  11.6 0.2 reduce-window.9
  11.8 0.7 broadcast_in_dim.25
  12.6 0.1 broadcast_in_dim_reshape.3.skip_ref
  12.7 0.7 bitcast_subtract_fusion
  13.4 0.1 pad_add_fusion.info_ref
  13.4 0.0 collective-permute-done.rim_x_ref.rim_b_ref.rim_c_ref
  13.4 0.0 copy-start
  13.4 1.7 copy-done
  15.2 0.0 copy-start.2
  15.2 0.9 copy-done.2
  16.1 0.0 copy-start.3
  16.1 0.8 copy-done.3
  16.9 0.0 copy-start.4
  16.9 0.8 copy-done.4
  17.6 0.0 copy-start.7
  17.6 0.7 copy-done.7
  18.3 9.2 %fresh_states.1 = (bf16[128,8192]{1,0:T(8,128)(2,1)S(1)}, bf16[8,2,128,128]{3,2,1,0:T(8,128)(2,1)S(1)}, bf16[8,128,1024]{2,1,0:T(8,128)(2,1)S(1)}, f32[8,8,1024]{2,1,0:T(8,128)S(1)}) custom-call(s32[7]{0:T(128)S(1)} %pad_add_fusion.info_ref, bf16[128,10240]{1,0:T(8,128)(2,1)S(1)} %bitcast.20, bf16[128,10240]{1,0:T(8,128)(2,1)S(1)} %bitcast.21, ...), custom_call_target="tpu_custom_call" | custom-call | flops 600000000 | bytes 8000000 | tf_op jit(solution)/shard_map/fresh_states/pallas_call | solution.py:324
  27.5 0.0 copy-start.1
  27.5 0.0 copy-start.5
  27.5 0.0 copy-start.6
  27.5 101.6 %hand_on_states.1.before_ref = bf16[8,128,1024]{2,1,0:T(8,128)(2,1)S(1)} custom-call(bf16[8,128,1024]{2,1,0:T(8,128)(2,1)S(1)} %get-tuple-element.8.fresh_ref, f32[8,8,1024]{2,1,0:T(8,128)S(1)} %get-tuple-element.9.through_ref), custom_call_target="tpu_custom_call" | custom-call | flops 10000000 | bytes 200000000 | tf_op jit(solution)/shard_map/hand_on_states/pallas_call | solution.py:363
  129.1 0.0 copy-done.1
  129.1 0.0 copy-done.5
  129.1 0.0 copy-done.6
  129.1 0.0 copy-start.10
  129.1 10.2 %mix_heads.1 = bf16[128,8192]{1,0:T(8,128)(2,1)} custom-call(s32[7]{0:T(128)S(1)} %pad_add_fusion.info_ref, bf16[128,8192]{1,0:T(8,128)(2,1)S(1)} %get-tuple-element.6.x_ref, bf16[8,2,128,128]{3,2,1,0:T(8,128)(2,1)S(1)} %get-tuple-element.7.proj_ref, bf16[8,128,1024]{2,1,0:T(8,128)(2,1)S(1)} %hand_on_states.1.before_ref, bf16[128,8192]{1,0:T(8,128)(2,1)S(1)} %bitcast.23, ...), custom_call_target="tpu_custom_call" | custom-call | flops 1000000000 | bytes 10000000 | tf_op jit(solution)/shard_map/mix_heads/pallas_call | solution.py:381
  139.3 0.0 all-gather.5.cloned.1.call-done
  139.3 0.0 all-gather.7.cloned.1.call-done
  139.3 0.0 copy-done.10
  139.3 0.0 copy-start.8
  139.3 2.2 %copy-done.8 = bf16[1,2048,1024]{2,1,0:T(8,128)(2,1)S(1)} copy-done((bf16[1,2048,1024]{2,1,0:T(8,128)(2,1)S(1)}, bf16[1,2048,1024]{2,1,0:T(8,128)(2,1)}, u32[]{:S(2)}) %copy-start.8) | copy-done | bytes 4194328
  141.5 0.0 copy-start.9
  141.5 2.2 %copy-done.9 = bf16[1,2048,1024]{2,1,0:T(8,128)(2,1)S(1)} copy-done((bf16[1,2048,1024]{2,1,0:T(8,128)(2,1)S(1)}, bf16[1,2048,1024]{2,1,0:T(8,128)(2,1)}, u32[]{:S(2)}) %copy-start.9) | copy-done | bytes 4194328
  143.7 38.8 %attend.1 = bf16[128,4096]{1,0:T(8,128)(2,1)} custom-call(s32[7]{0:T(128)S(1)} %pad_add_fusion.info_ref, bf16[128,4096]{1,0:T(8,128)(2,1)S(1)} %bitcast.34, bf16[2048,1024]{1,0:T(8,128)(2,1)S(1)} %bitcast.32, bf16[2048,1024]{1,0:T(8,128)(2,1)S(1)} %bitcast.33), custom_call_target="tpu_custom_call" | custom-call | flops 4000000000 | bytes 10000000 | tf_op jit(solution)/shard_map/attend/pallas_call | solution.py:412
Async XLA Ops:
  7.2 132.2 %all-gather.5.cloned.1.call-start = ((), (), s32[]{:S(2)}) async-start(), calls=%async_computation | async-start | bytes 4456448 | tf_op jit(solution)/shard_map/all_gather | solution.py:297
  7.9 131.4 %all-gather.7.cloned.1.call-start = ((), (), s32[]{:S(2)}) async-start(), calls=%async_computation.1 | async-start | bytes 4456448 | tf_op jit(solution)/shard_map/all_gather | solution.py:298
  9.6 3.8 %collective-permute-start = (bf16[16,10240]{1,0:T(8,128)(2,1)S(1)}, bf16[16,10240]{1,0:T(8,128)(2,1)S(1)}, u32[]{:S(2)}, u32[]{:S(2)}) collective-permute-start(bf16[16,10240]{1,0:T(8,128)(2,1)S(1)} %slice_bitcast_fusion), channel_id=1, source_target_pairs={{0,2},{2,4},{4,6},{6,8},{8,10},{10,12},{12,14},{14,16},{16,18},{18... | collective-permute-start | bytes 983048 | tf_op jit(solution)/shard_map/ppermute | solution.py:299
  13.4 1.7 copy-start
  15.2 0.9 copy-start.2
  16.1 0.8 copy-start.3
  16.9 0.8 copy-start.4
  17.6 0.7 copy-start.7
  27.5 101.6 %copy-start.1 = (bf16[1,128,8192]{2,1,0:T(8,128)(2,1)S(1)}, bf16[1,128,8192]{2,1,0:T(8,128)(2,1)}, u32[]{:S(2)}) copy-start(bf16[1,128,8192]{2,1,0:T(8,128)(2,1)} %param.13) | copy-start | bytes 6291460
  27.5 101.6 %copy-start.5 = (bf16[1,128,128]{2,1,0:T(8,128)(2,1)S(1)}, bf16[1,128,128]{2,1,0:T(8,128)(2,1)}, u32[]{:S(2)}) copy-start(bf16[1,128,128]{2,1,0:T(8,128)(2,1)} %param.14) | copy-start | bytes 98308
  27.5 101.6 %copy-start.6 = (f32[8192]{0:T(1024)S(1)}, f32[8192]{0:T(1024)}, u32[]{:S(2)}) copy-start(f32[8192]{0:T(1024)} %param.19) | copy-start | bytes 98308
  129.1 10.2 %copy-start.10 = (bf16[1,128,4096]{2,1,0:T(8,128)(2,1)S(1)}, bf16[1,128,4096]{2,1,0:T(8,128)(2,1)}, u32[]{:S(2)}) copy-start(bf16[1,128,4096]{2,1,0:T(8,128)(2,1)} %param.21) | copy-start | bytes 3145732
  139.3 2.2 %copy-start.8 = (bf16[1,2048,1024]{2,1,0:T(8,128)(2,1)S(1)}, bf16[1,2048,1024]{2,1,0:T(8,128)(2,1)}, u32[]{:S(2)}) copy-start(bf16[1,2048,1024]{2,1,0:T(8,128)(2,1)} %all-gather.5.cloned.1.call-done) | copy-start | bytes 12582916
  141.5 2.2 %copy-start.9 = (bf16[1,2048,1024]{2,1,0:T(8,128)(2,1)S(1)}, bf16[1,2048,1024]{2,1,0:T(8,128)(2,1)}, u32[]{:S(2)}) copy-start(bf16[1,2048,1024]{2,1,0:T(8,128)(2,1)} %all-gather.7.cloned.1.call-done) | copy-start | bytes 12582916
Sparse Core Ops, SparseCore 0:
  10.2 51.2 all-gather.4
  63.6 58.6 all-gather.6
